TPU v7x, 512 devices: a whole 4x4x16 slice. The times are simulated.
512 devices in a mesh: dp: 64 (over y_hi, z, core), tensor: 8 (over x, y_lo).
Axes of the slice: x: 4, y: 4 (y_hi: 2, y_lo: 2; y = y_hi * 2 + y_lo), z: 16, core: 2. Of those that a mesh axis runs over, the one named last changes fastest.
Arguments:
- hidden: bfloat16 [16384, 8192], P('dp', 'tensor'), may hold values from -600 to 600, as said below
- norm_gain: bfloat16 [8192], replicated, may hold values from 0.099609375 to 1.8984375
- query_weight: bfloat16 [8192, 4096], P(('dp', 'tensor')), may hold values from -0.0625 to 0.0625
- key_weight: bfloat16 [8192, 1024], P(('dp', 'tensor')), may hold values from -0.0625 to 0.0625
- value_weight: bfloat16 [8192, 1024], P(('dp', 'tensor')), may hold values from -0.0625 to 0.0625
- query_bias: bfloat16 [4096], P('tensor'), may hold values from -2 to 8, as said below
- key_bias: bfloat16 [1024], P('tensor'), may hold values from -2 to 6, as said below
- value_bias: bfloat16 [1024], P('tensor'), may hold values from -3 to 3
- lengths: int32 [64, 4], P('dp'), may hold values from 1 to 128, 256 in all within a row
- page_table: int32 [64, 16], P('dp'), may hold values from 0 to 15, each once within a row
Outputs:
- attention: bfloat16 [16384, 4096], P('dp', 'tensor')
- cache_pages: bfloat16 [1024, 32, 2048], P('dp', None, 'tensor')
Inputs may be any that keep to these rules, and one draw needn't show every extreme that they name: `hidden`: the custom draw of the layer input. `query_bias`: the custom draw of the query bias. `key_bias`: the custom draw of the key bias. Each replica's lengths sum to 256, and its longest rollout has exactly 128 tokens. `page_table`: each replica's row is a permutation of its 16 pages.
All inputs are finite; a program needn't handle non-finite values.
Results may differ from a plain program's by a relative error of at most 0.0088.
Values may be sent and summed in bfloat16 or wider, within the bound.
A program may use at most 64 MiB of HBM per device.

v0:
```python
import jax
import jax.numpy as jnp
from jax import lax
from jax.sharding import PartitionSpec as P

HD = 128
ROLLS = 4
PAGE = 32
BLOCKS = 4
PAGES_REP = 16


rope_base = 1000000.0


def rotary(values_f, positions):
    halfway = HD // 2
    frequency = rope_base ** (-(jnp.arange(halfway, dtype=jnp.float32) * 2.0 / HD))
    angles = positions.astype(jnp.float32)[:, None] * frequency[None, :]
    cosine = jnp.cos(angles)[:, None, :]
    sine_part = jnp.sin(angles)[:, None, :]
    lower_half = values_f[..., :halfway]
    upper_half = values_f[..., halfway:]
    return jnp.concatenate(
        [
            lower_half * cosine - upper_half * sine_part,
            upper_half * cosine + lower_half * sine_part,
        ],
        axis=-1,
    )


def segments_of(length_row, token_count):
    ends = jnp.cumsum(length_row)
    starts = ends - length_row
    tok_index = jnp.arange(token_count, dtype=jnp.int32)
    segment = jnp.sum((tok_index[None, :] >= ends[:, None]).astype(jnp.int32), axis=0)
    onehot = segment[:, None] == jnp.arange(ROLLS, dtype=jnp.int32)[None, :]
    leading = jnp.sum(jnp.where(onehot, starts[None, :], 0), axis=1)
    return (segment, tok_index - leading, starts)


def attention_of(queries, key_rows, value_rows, segment):
    token_count = queries.shape[0]
    kv_heads = key_rows.shape[1]
    group_size = queries.shape[1] // kv_heads
    grouped = queries.reshape(token_count, kv_heads, group_size, HD)
    scores = jnp.einsum(
        "ikgd,jkd->kgij", grouped, key_rows, preferred_element_type=jnp.float32
    ) * HD ** (-0.5)
    tok_index = jnp.arange(token_count, dtype=jnp.int32)
    allowed = (segment[:, None] == segment[None, :]) & (tok_index[None, :] <= tok_index[:, None])
    scores = jnp.where(allowed[None, None], scores, -1e30)
    row_max = jnp.max(scores, axis=-1, keepdims=True)
    weights = jnp.exp(scores - row_max)
    weights = (weights / jnp.sum(weights, axis=-1, keepdims=True)).astype(jnp.bfloat16)
    mixed = jnp.einsum("kgij,jkd->ikgd", weights, value_rows, preferred_element_type=jnp.float32)
    return mixed.reshape(token_count, kv_heads * group_size * HD).astype(jnp.bfloat16)


def pages_of(kv_rows, length_row, starts, page_row):
    slots = jnp.arange(PAGES_REP, dtype=jnp.int32)
    owner = slots // BLOCKS
    within = slots % BLOCKS
    offsets = within[:, None] * PAGE + jnp.arange(PAGE, dtype=jnp.int32)[None, :]
    onehot = owner[:, None] == jnp.arange(ROLLS, dtype=jnp.int32)[None, :]
    owner_len = jnp.sum(jnp.where(onehot, length_row[None, :], 0), axis=1)
    owner_start = jnp.sum(jnp.where(onehot, starts[None, :], 0), axis=1)
    valid_slot = offsets < owner_len[:, None]
    source = jnp.where(valid_slot, owner_start[:, None] + offsets, 0)
    blocks_out = jnp.where(valid_slot[..., None], kv_rows[source], jnp.zeros((), jnp.bfloat16))
    empty = jnp.zeros((PAGES_REP, PAGE, kv_rows.shape[1]), jnp.bfloat16)
    return empty.at[page_row].set(blocks_out)


def column_slice(whole, parts_count, rank_index):
    width = whole.shape[1] // parts_count
    return lax.dynamic_slice_in_dim(whole, rank_index * width, width, 1)


def on_device(
    hidden,
    norm_gain,
    query_weight,
    key_weight,
    value_weight,
    query_bias,
    key_bias,
    value_bias,
    lengths,
    page_table,
):
    tokens = lax.all_gather(hidden, "tensor", axis=1, tiled=True)
    token_count = tokens.shape[0]
    tokens_f = tokens.astype(jnp.float32)
    meansq = jnp.mean(tokens_f * tokens_f, axis=-1, keepdims=True)
    normed = (tokens_f * lax.rsqrt(meansq + 1e-06) * norm_gain.astype(jnp.float32)).astype(
        jnp.bfloat16
    )
    length_row = lengths[0]
    segment, position, starts = segments_of(length_row, token_count)
    whole_query, whole_key, whole_value = (
        lax.all_gather(query_weight, "tensor", axis=0, tiled=True),
        lax.all_gather(key_weight, "tensor", axis=0, tiled=True),
        lax.all_gather(value_weight, "tensor", axis=0, tiled=True),
    )
    group_count = lax.axis_size("tensor")
    rank_index = lax.axis_index("tensor")
    local_query = column_slice(whole_query, group_count, rank_index)
    local_key = column_slice(whole_key, group_count, rank_index)
    local_value = column_slice(whole_value, group_count, rank_index)

    def add_rows(shard_rows):
        return jnp.dot(normed, shard_rows, preferred_element_type=jnp.float32)

    shard_rows = (
        lax.all_gather(local_query, "dp", axis=0, tiled=True),
        lax.all_gather(local_key, "dp", axis=0, tiled=True),
        lax.all_gather(local_value, "dp", axis=0, tiled=True),
    )
    proj_query = add_rows(shard_rows[0])
    proj_key = add_rows(shard_rows[1])
    proj_value = add_rows(shard_rows[2])
    kv_heads = proj_key.shape[1] // HD
    q_heads = proj_query.shape[1] // HD
    key_rows = rotary(
        (proj_key + key_bias.astype(jnp.float32)).reshape(token_count, kv_heads, HD), position
    ).astype(jnp.bfloat16)
    value_rows = (
        (proj_value + value_bias.astype(jnp.float32))
        .astype(jnp.bfloat16)
        .reshape(token_count, kv_heads, HD)
    )
    kv_rows = jnp.stack([key_rows, value_rows], axis=2).reshape(token_count, kv_heads * 2 * HD)
    cache_pages = pages_of(kv_rows, length_row, starts, page_table[0])
    queries = rotary(
        (proj_query + query_bias.astype(jnp.float32)).reshape(token_count, q_heads, HD), position
    ).astype(jnp.bfloat16)
    attention = attention_of(queries, key_rows, value_rows, segment)
    return (attention, cache_pages)


def solution(mesh):
    placed = (
        P("dp", "tensor"),
        P(),
        P(("dp", "tensor"), None),
        P(("dp", "tensor"), None),
        P(("dp", "tensor"), None),
        P("tensor"),
        P("tensor"),
        P("tensor"),
        P("dp", None),
        P("dp", None),
    )
    return jax.shard_map(
        on_device,
        mesh=mesh,
        in_specs=placed,
        out_specs=(P("dp", "tensor"), P("dp", None, "tensor")),
        check_vma=False,
    )
```

profile of v0, /device:TPU:1, one launch (start us, length us, event | category | flops | bytes accessed | tf_op | source)
XLA Modules:
  0.0 634.6 jit_solution(7657329097963163493)
XLA Ops:
  7.2 0.0 all-gather.12.cloned.1.call-start
  7.2 0.7 all-gather.12.cloned.1.call-update
  7.9 0.0 all-gather.6.cloned.1.call-start
  7.9 0.7 all-gather.6.cloned.1.call-update
  8.6 0.0 all-gather.10.cloned.1.call-start
  8.7 23.3 %all_gather.24 = bf16[128,1024]{1,0:T(8,128)(2,1)S(1)} all-gather(bf16[16,1024]{1,0:T(8,128)(2,1)} %param.13), channel_id=1, replica_groups=mesh['dp'=64,'tensor'=8] {'tensor'}, dimensions={0}, use_global_device_ids=true | all-gather | bytes 294912 | tf_op jit(solution)/shard_map/all_gather | solution.py:104
  32.0 0.6 constant_dynamic-slice_fusion.1
  32.6 0.0 all-gather.8.cloned.1.call-start
  32.7 24.8 %all_gather.22 = bf16[128,1024]{1,0:T(8,128)(2,1)S(1)} all-gather(bf16[16,1024]{1,0:T(8,128)(2,1)} %param.14), channel_id=1, replica_groups=mesh['dp'=64,'tensor'=8] {'tensor'}, dimensions={0}, use_global_device_ids=true | all-gather | bytes 294912 | tf_op jit(solution)/shard_map/all_gather | solution.py:105
  57.5 0.6 constant_dynamic-slice_fusion.2
  58.1 0.0 all-gather.14.cloned.1.call-start
  58.2 1.9 all-gather.12.cloned.1.call-done
  60.1 1.6 constant_dynamic-slice_fusion
  61.7 0.7 convert_element_type.62
  62.4 0.7 convert_element_type.69
  63.1 0.8 broadcast_in_dim.62
  63.9 0.7 convert_element_type.67
  64.6 0.7 convert_element_type.64
  65.2 0.7 fusion.27
  65.9 0.7 select_reduce_fusion.2
  66.6 0.1 compare_select_fusion
  66.7 0.1 reshape.441
  66.8 0.1 convert_reduce_fusion
  66.9 0.1 select_reduce_fusion
  67.0 0.7 fusion.26
  67.6 0.1 add_compare_fusion
  67.7 0.1 fusion.12
  67.8 0.5 multiply_cosine_fusion
  68.4 94.6 %all-gather.6.cloned.1.call-done = bf16[256,8192]{1,0:T(8,128)(2,1)} async-done(((bf16[256,1024]{1,0:T(8,128)(2,1)}), bf16[256,8192]{1,0:T(8,128)(2,1)}) %all-gather.6.cloned.1.call-update) | async-done | bytes 4194320 | tf_op jit(solution)/shard_map/all_gather | solution.py:93
  163.0 3.1 fusion
  166.1 147.7 %all-gather.10.cloned.1.call-done = bf16[8192,128]{1,0:T(8,128)(2,1)} async-done(((bf16[128,128]{1,0:T(8,128)(2,1)}), bf16[8192,128]{1,0:T(8,128)(2,1)}) %all-gather.10.cloned.1.call-update) | async-done | bytes 2097168 | tf_op jit(solution)/shard_map/all_gather | solution.py:118
  313.8 4.6 fusion.5
  318.4 0.3 fusion.18
  318.7 136.4 %all-gather.8.cloned.1.call-done = bf16[8192,128]{1,0:T(8,128)(2,1)} async-done(((bf16[128,128]{1,0:T(8,128)(2,1)}), bf16[8192,128]{1,0:T(8,128)(2,1)}) %all-gather.8.cloned.1.call-update) | async-done | bytes 2097168 | tf_op jit(solution)/shard_map/all_gather | solution.py:119
  455.2 4.6 fusion.6
  459.8 0.1 copy.28
  459.9 2.0 gather_fusion
  461.9 0.1 broadcast_select_fusion
  462.0 1.0 scatter_fusion
  463.1 155.4 %all-gather.14.cloned.1.call-done = bf16[8192,512]{1,0:T(8,128)(2,1)} async-done(((bf16[128,512]{1,0:T(8,128)(2,1)}), bf16[8192,512]{1,0:T(8,128)(2,1)}) %all-gather.14.cloned.1.call-update) | async-done | bytes 8388624 | tf_op jit(solution)/shard_map/all_gather | solution.py:117
  618.5 7.0 %convolution_add_fusion = f32[256,512]{1,0:T(8,128)S(1)} fusion(bf16[8192,512]{1,0:T(8,128)(2,1)} %all-gather.14.cloned.1.call-done, f32[512]{0:T(512)S(1)} %convert_element_type.69, bf16[256,8192]{1,0:T(8,128)(2,1)} %all-gather.6.cloned.1.call-done, f32[8192]{0:T(1024)S(1)} %convert_element_type.62, f32[256]{0:T(256)S(1)} %add_rsqrt_fusion), kind=kOutput, calls=%fused_computation.10 | convolution fusion | flops 2156003328 | bytes 13143040 | tf_op jit(solution)/shard_map/dot_general | solution.py:114
  625.6 0.2 reshape.436
  625.8 0.3 fusion.32
  626.1 0.1 subtract_convert_fusion
  626.2 0.4 fusion.33
  626.7 0.2 fusion.7
  626.8 0.3 convolution_convert_fusion
  627.2 0.8 copy.29
  (12 shorter events, 0.1 us)
Async XLA Ops:
  7.2 52.9 %all-gather.12.cloned.1.call-start = ((), (), s32[]{:S(2)}) async-start(), calls=%async_computation.3 | async-start | bytes 1179648 | tf_op jit(solution)/shard_map/all_gather | solution.py:103
  7.9 155.1 %all-gather.6.cloned.1.call-start = ((), (), s32[]{:S(2)}) async-start(), calls=%async_computation | async-start | bytes 4718592 | tf_op jit(solution)/shard_map/all_gather | solution.py:93
  8.6 305.1 %all-gather.10.cloned.1.call-start = ((), (), s32[]{:S(2)}) async-start(), calls=%async_computation.2 | async-start | bytes 2129920 | tf_op jit(solution)/shard_map/all_gather | solution.py:118
  32.6 422.6 %all-gather.8.cloned.1.call-start = ((), (), s32[]{:S(2)}) async-start(), calls=%async_computation.1 | async-start | bytes 2129920 | tf_op jit(solution)/shard_map/all_gather | solution.py:119
  58.1 560.4 %all-gather.14.cloned.1.call-start = ((), (), s32[]{:S(2)}) async-start(), calls=%async_computation.4 | async-start | bytes 8519680 | tf_op jit(solution)/shard_map/all_gather | solution.py:117
  463.1 162.5 %copy-start = (bf16[16,32,256]{2,1,0:T(8,128)(2,1)}, bf16[16,32,256]{2,1,0:T(8,128)(2,1)S(1)}, u32[]{:S(2)}) copy-start(bf16[16,32,256]{2,1,0:T(8,128)(2,1)S(1)} %scatter_fusion) | copy-start | bytes 786436
Sparse Core Ops, SparseCore 0:
  10.1 49.9 all-gather.11
  62.2 100.7 all-gather.5
  166.8 146.8 all-gather.9
  316.9 138.1 all-gather.7
  458.9 159.5 all-gather.13
where the time goes:
time: 635 us
  waiting for transfers between devices  538 us (85%)
  blocking collectives  48.1 us (8%)
  matrix products  17 us (3%)
  between operations  13.9 us (2%)
  other arithmetic  10.5 us (2%)
  local copies, waits for them, and re-layouts  7.36 us (1%)
    all_gather x1, waiting for transfers between devices, on_device(): lax.all_gather(local_query, 'dp', axis=0, tiled=True)  155 us
    all_gather x1, waiting for transfers between devices, on_device(): lax.all_gather(local_key, 'dp', axis=0, tiled=True)  148 us
    all_gather x1, waiting for transfers between devices, on_device(): lax.all_gather(local_value, 'dp', axis=0, tiled=True)  136 us
    all_gather x1, waiting for transfers between devices, on_device(): tokens = lax.all_gather(hidden, 'tensor', axis=1, tiled=True)  94.6 us
    all_gather x1, blocking collectives, on_device(): lax.all_gather(value_weight, 'tensor', axis=0, tiled=True)  24.8 us
    all_gather x1, blocking collectives, on_device(): lax.all_gather(key_weight, 'tensor', axis=0, tiled=True)  23.3 us
    dot_general x3, matrix products, add_rows(): return jnp.dot(normed, shard_rows, preferred_element_type=jnp.float32)  16.3 us
  transfers between devices with their start and end apart: 5, of which 5 were waited for; matrix products, arithmetic and copies ran while one was open for 4% of the time, Pallas kernels for 0%

commit v1 on v0

v1 whole, which is shorter than its diff:
```python
import functools
import math

import jax
import jax.numpy as jnp
from jax import lax
from jax.experimental import pallas as pl
from jax.experimental.pallas import tpu as pltpu
from jax.sharding import PartitionSpec as P

MESH = pl.DeviceIdType.MESH
HD = 128
ROLLS = 4
PAGE = 32
BLOCKS = 4
PAGES_REP = 16
TOK = 256
D = 8192
NZ = 16
BASE = 1000000.0
F32 = jnp.float32
BF16 = jnp.bfloat16
NEG = -1e30


def rem(a, n):
    return lax.rem(a, n)


def kernel(
    h_ref, gain_ref, wq_ref, wk_ref, wv_ref, bq_ref, bk_ref, bv_ref, len_ref, pt_ref,
    att_ref, page_ref,
    ws, wb, hs, a5, a2, ps, rs, ssb, cos_t, sin_t, mask_t, hot_t, kv_t,
    ws_send, ws_send_self, ws_recv, z_send, z_recv, c_send, c_recv, h_send, h_recv, p_send, p_recv, s_send, s_recv,
):
    dp = lax.axis_index("dp")
    t = lax.axis_index("tensor")
    y_hi, z, core = dp // (2 * NZ), rem(dp // 2, NZ), rem(dp, 2)
    x, y_lo = t // 2, rem(t, 2)

    def dev(x, y_lo, y_hi, z, core):
        return ((y_hi * NZ + z) * 2 + core, x * 2 + y_lo)

    def flip(bit, by):
        return rem(bit + by, 2)

    barrier = pltpu.get_barrier_semaphore()
    peers = []
    for r in range(1, 32):
        peers.append(dev(rem(x + r % 4, 4), flip(y_lo, r // 4 % 2), flip(y_hi, r // 8 % 2), z, flip(core, r // 16)))
    up, down = rem(z + 1, NZ), rem(z + NZ - 1, NZ)
    up_dev, down_dev = dev(x, y_lo, y_hi, up, core), dev(x, y_lo, y_hi, down, core)
    peers += [up_dev, down_dev]
    for d in peers:
        pl.semaphore_signal(barrier, inc=1, device_id=d, device_id_type=MESH)

    g = gain_ref[...].astype(F32)
    g_row = jnp.sum(jnp.where(lax.broadcasted_iota(jnp.int32, g.shape, 0) == dp, g, 0.0), axis=0, keepdims=True)
    lane = lax.broadcasted_iota(jnp.int32, (16, 128), 1)
    sub = lax.broadcasted_iota(jnp.int32, (16, 128), 0)
    g_col = jnp.sum(jnp.where(lane == sub + 16 * t, g_row, 0.0), axis=1, keepdims=True)
    for yh_d in range(2):
        for yl_d in range(2):
            for k in range(2):
                for e in range(2):
                    td = 4 * k + 2 * e + yl_d
                    first = (wk_ref if yh_d == 0 else wv_ref)[:, 128 * td : 128 * td + 128]
                    q0 = 512 * td + 256 * yh_d
                    parts = (first, wq_ref[:, q0 : q0 + 128], wq_ref[:, q0 + 128 : q0 + 256])
                    for j in range(3):
                        ws[(yh_d * 2 + yl_d) * 2 + k, j, :, 128 * e : 128 * e + 128] = (
                            parts[j].astype(F32) * g_col
                        ).astype(BF16)
    for b in range(2):
        for u in range(4):
            hs[b, u] = h_ref[:, 256 * u + 128 * b : 256 * u + 128 * b + 128]

    pl.semaphore_wait(barrier, len(peers))

    def remote(src, dst, send, recv, device):
        pltpu.make_async_remote_copy(
            src_ref=src, dst_ref=dst, send_sem=send, recv_sem=recv, device_id=device, device_id_type=MESH
        ).start()

    def wait(ref, sem):
        pltpu.make_async_copy(ref, ref, sem).wait()

    x_dst = 2 * y_hi + core
    slot_w = pl.ds(pl.multiple_of(16 * t, 16), 16)
    for r in range(8):
        yl_d, yh_d, k = flip(y_lo, r % 2), flip(y_hi, r // 2 % 2), flip(core, r // 4)
        src = ws.at[(yh_d * 2 + yl_d) * 2 + k]
        dst = wb.at[:, k, slot_w, :]
        to = dev(x_dst, yl_d, yh_d, z, k)
        if r > 0:
            remote(src, dst, ws_send, ws_recv, to)
        else:

            @pl.when(x == x_dst)
            def _():
                pltpu.make_async_copy(src, dst, ws_recv).start()

            @pl.when(x != x_dst)
            def _():
                remote(src, dst, ws_send_self, ws_recv, to)

    xb = rem(x, 2)
    x_pair = x + 1 - 2 * xb
    piece = 4 * (y_hi * 4 + rem(t, 4))
    for r in (1, 2, 3, 4, 5, 6, 7):
        xd = x if r < 4 else x_pair
        src = hs.at[xb if r < 4 else 1 - xb]
        to = dev(xd, flip(y_lo, r % 2), flip(y_hi, r // 2 % 2), z, core)
        remote(src, a5.at[pl.ds(piece, 4)], h_send, h_recv, to)
    for u in range(4):
        a5[piece + u] = hs[xb, u]

    me = core
    other = 1 - core

    def rows(p, half, lo=0, n=128):
        return pl.ds(p * 256 + half * 128 + lo, n)

    def z_copy(way, j, src_rows, dst_rows, sub_id, step):
        remote(
            wb.at[j, me, src_rows, :], wb.at[j, me, dst_rows, :], z_send, z_recv.at[way, sub_id, step - 1],
            up_dev if way == 0 else down_dev,
        )

    def to_core(j, at):
        remote(wb.at[j, me, at, :], wb.at[j, me, at, :], c_send, c_recv.at[j], dev(x, y_lo, y_hi, z, other))

    wait(wb.at[:, me, rows(0, 0), :], ws_recv)
    for j in range(2):
        for way in range(2):
            z_copy(way, j, rows(0, 0), rows(1, way), j, 1)

    h = h_ref[...].astype(F32)
    sq = h * h
    hi = sq.astype(BF16)
    lo = (sq - hi.astype(F32)).astype(BF16)
    ones = jnp.ones((8, 1024), BF16)
    nt = (((1,), (1,)), ((), ()))
    ssb[0] = lax.dot_general(ones, hi, nt, preferred_element_type=F32) + lax.dot_general(
        ones, lo, nt, preferred_element_type=F32
    )
    for r in range(1, 8):
        remote(ssb.at[0], ssb.at[r], s_send, s_recv, dev(rem(x + r % 4, 4), flip(y_lo, r // 4), y_hi, z, core))
    for j in range(3):
        to_core(j, rows(0, 0))

    def first_tables():
        ends, starts, total = [], [], 0
        for r in range(ROLLS):
            starts.append(total)
            total = total + len_ref[0, r]
            ends.append(total)
        tok = lax.broadcasted_iota(jnp.int32, (TOK, 128), 0)
        begin = jnp.zeros((TOK, 128), jnp.int32)
        for r in range(1, ROLLS):
            begin = jnp.where(tok >= ends[r - 1], starts[r], begin)
        d = lax.broadcasted_iota(jnp.int32, (TOK, 128), 1)
        half = rem(d, 64).astype(F32)
        freq = jnp.exp(half * (-2.0 / HD * math.log(BASE)))
        angle = (tok - begin).astype(F32) * freq
        cos_t[...] = jnp.cos(angle)
        s = jnp.sin(angle)
        sin_t[...] = jnp.where(d < 64, -s, s)
        for q in range(2):
            col = d + 128 * q
            mask_t[:, 128 * q : 128 * q + 128] = jnp.where((col >= begin) & (col <= tok), 0.0, NEG)

    def page_tables():
        ends, starts, total = [], [], 0
        for r in range(ROLLS):
            starts.append(total)
            total = total + len_ref[0, r]
        n = lax.broadcasted_iota(jnp.int32, (PAGES_REP * PAGE, 128), 0)
        page, slot = n // PAGE, rem(n, PAGE)
        src = jnp.full(n.shape, -1, jnp.int32)
        for e in range(PAGES_REP):
            r, b = e // BLOCKS, e % BLOCKS
            at = b * PAGE + slot
            src = jnp.where((page == pt_ref[0, e]) & (at < len_ref[0, r]), starts[r] + at, src)
        col = lax.broadcasted_iota(jnp.int32, (PAGES_REP * PAGE, 128), 1)
        for q in range(2):
            hot_t[:, 128 * q : 128 * q + 128] = jnp.where(src == col + 128 * q, 1.0, 0.0).astype(BF16)

    def wait_hidden():
        wait(a5.at[pl.ds(0, 28)], h_recv)

    def relay(tk):
        for p in range(8):
            m1 = rem(z + NZ - p, NZ)
            m2 = rem(z + p, NZ) if p else rem(z + 8, NZ)
            a2[tk, :, 256 * p : 256 * p + 128] = a5[tk * NZ + m1]
            a2[tk, :, 256 * p + 128 : 256 * p + 256] = a5[tk * NZ + m2]

    def product(j, k):
        if k == 0:
            wait(wb.at[j, other], c_recv.at[j])

        @pl.loop(0, 2)
        def _(tk):
            part = jnp.dot(a2[tk], wb[j, k], preferred_element_type=F32).astype(BF16)
            for e in range(2):
                ps[j, tk * 4 + 2 * k + e] = part[:, 128 * e : 128 * e + 128]

    def send_parts(j):
        for r in range(7, 0, -1):
            xd, yh_d = rem(x + r % 4, 4), flip(y_hi, r // 4)
            remote(ps.at[j, yh_d * 4 + xd], rs.at[j, r], p_send, p_recv.at[j], dev(xd, y_lo, yh_d, z, core))

    def both(tasks):
        def run():
            for f in tasks:
                f()

        return run

    P_ = functools.partial
    groups = (
        ([(0, 0, 128), (1, 0, 128)], {1: first_tables, 3: page_tables}),
        (
            [(2, 0, 64), (2, 64, 64)],
            {
                1: both([wait_hidden, P_(relay, 0)]),
                2: both([P_(relay, 1), P_(product, 0, 0)]),
                3: both([P_(product, 0, 1), P_(send_parts, 0)]),
                4: P_(product, 1, 0),
                5: both([P_(product, 1, 1), P_(send_parts, 1)]),
            },
        ),
    )
    for gi, (subs, tasks) in enumerate(groups):
        for step in range(1, 9):
            for si, (j, lo_row, n) in enumerate(subs):
                for way in range(2):
                    sem = z_recv.at[way, 2 * gi + si, step - 1]
                    if step < 8:
                        at = rows(step, way, lo_row, n)
                        wait(wb.at[j, me, at, :], sem)
                        if step < 7:
                            z_copy(way, j, at, rows(step + 1, way, lo_row, n), 2 * gi + si, step + 1)
                        elif gi == 0 or way == si:
                            half = way * 64
                            z_copy(way, j, rows(7, way, half, 64), rows(0, 1, half, 64), 2 * gi + si, 8)
                        to_core(j, at)
                    elif gi == 0 or way == si:
                        at = rows(0, 1, way * 64, 64)
                        wait(wb.at[j, me, at, :], sem)
                        to_core(j, at)
            if step == 7 and gi == 0:
                for si, (j, lo_row, n) in enumerate(groups[1][0]):
                    for way in range(2):
                        z_copy(way, j, rows(0, 0, lo_row, n), rows(1, way, lo_row, n), 2 + si, 1)
            if step in tasks:
                tasks[step]()
    product(2, 0)
    product(2, 1)
    send_parts(2)

    wait(ssb.at[pl.ds(1, 7)], s_recv)
    total = ssb[0, 0:1, :]
    for r in range(1, 8):
        total = total + ssb[r, 0:1, :]
    scale_row = lax.rsqrt(total * (1.0 / D) + 1e-6)
    eye = lax.broadcasted_iota(jnp.int32, (TOK, TOK), 0) == lax.broadcasted_iota(jnp.int32, (TOK, TOK), 1)
    scale = jnp.sum(jnp.where(eye, scale_row, 0.0), axis=1, keepdims=True)

    def gathered(j):
        wait(rs.at[j, pl.ds(1, 7)], p_recv.at[j])
        own = ps[j, y_hi * 4 + x].astype(F32)
        for r in range(1, 4):
            own = own + rs[j, r].astype(F32)
        far = rs[j, 4].astype(F32)
        for r in range(5, 8):
            far = far + rs[j, r].astype(F32)
        return (
            jnp.where(y_hi == 0, own, far) * scale,
            jnp.where(y_hi == 0, far, own) * scale,
        )

    def rope(v):
        return (v * cos_t[...] + pltpu.roll(v, 64, 1) * sin_t[...]).astype(BF16)

    key, value = gathered(0)
    key = rope(key + bk_ref[...].astype(F32))
    value = (value + bv_ref[...].astype(F32)).astype(BF16)
    kv_t[:, 0:128] = key
    kv_t[:, 128:256] = value
    page_ref[...] = jnp.dot(hot_t[...], kv_t[...], preferred_element_type=F32).astype(BF16)

    def attend(head, q):
        q = rope(q + bq_ref[:, 128 * head : 128 * head + 128].astype(F32))
        s = lax.dot_general(q, kv_t[:, 0:128], nt, preferred_element_type=F32) * HD ** (-0.5) + mask_t[...]
        w = jnp.exp(s - jnp.max(s, axis=-1, keepdims=True))
        w = (w / jnp.sum(w, axis=-1, keepdims=True)).astype(BF16)
        att_ref[:, 128 * head : 128 * head + 128] = jnp.dot(
            w, kv_t[:, 128:256], preferred_element_type=F32
        ).astype(BF16)

    for j in (1, 2):
        low, high = gathered(j)
        attend(j - 1, low)
        attend(j + 1, high)

    wait(ws.at[pl.ds(0, 7)], ws_send)

    @pl.when(x != x_dst)
    def _():
        wait(ws.at[0], ws_send_self)

    wait(a5.at[pl.ds(0, 28)], h_send)
    wait(ssb.at[pl.ds(1, 7)], s_send)
    wait(wb.at[:, 0, pl.ds(0, 1920), :], z_send)
    wait(wb.at[:, 0], c_send)
    wait(rs.at[:, pl.ds(1, 7)], p_send)


def on_device(hidden, gain, wq, wk, wv, bq, bk, bv, lengths, table):
    vmem = pl.BlockSpec(memory_space=pltpu.VMEM)
    smem = pl.BlockSpec(memory_space=pltpu.SMEM)
    dma = pltpu.SemaphoreType.DMA
    att, pages = pl.pallas_call(
        kernel,
        out_shape=(
            jax.ShapeDtypeStruct((TOK, 4 * HD), BF16),
            jax.ShapeDtypeStruct((PAGES_REP * PAGE, 2 * HD), BF16),
        ),
        in_specs=[vmem] * 8 + [smem] * 2,
        out_specs=(vmem, vmem),
        scratch_shapes=[
            pltpu.VMEM((8, 3, 16, 256), BF16),
            pltpu.VMEM((3, 2, 2048, 256), BF16),
            pltpu.VMEM((2, 4, TOK, 128), BF16),
            pltpu.VMEM((32, TOK, 128), BF16),
            pltpu.VMEM((2, TOK, 2048), BF16),
            pltpu.VMEM((3, 8, TOK, 128), BF16),
            pltpu.VMEM((3, 8, TOK, 128), BF16),
            pltpu.VMEM((8, 8, TOK), F32),
            pltpu.VMEM((TOK, 128), F32),
            pltpu.VMEM((TOK, 128), F32),
            pltpu.VMEM((TOK, TOK), F32),
            pltpu.VMEM((PAGES_REP * PAGE, TOK), BF16),
            pltpu.VMEM((TOK, 256), BF16),
            dma, dma, dma, dma, dma((2, 4, 8)), dma, dma((3,)), dma, dma, dma, dma((3,)), dma, dma,
        ],
        compiler_params=pltpu.CompilerParams(
            collective_id=0, has_side_effects=True, vmem_limit_bytes=40 * 2**20
        ),
        name="handover",
    )(
        hidden, gain.reshape(64, 128), wq, wk, wv, bq.reshape(1, -1), bk.reshape(1, -1), bv.reshape(1, -1),
        lengths, table,
    )
    return att, pages.reshape(PAGES_REP, PAGE, 2 * HD)


def solution(mesh):
    placed = (
        P("dp", "tensor"),
        P(),
        P(("dp", "tensor"), None),
        P(("dp", "tensor"), None),
        P(("dp", "tensor"), None),
        P("tensor"),
        P("tensor"),
        P("tensor"),
        P("dp", None),
        P("dp", None),
    )
    return jax.shard_map(
        on_device,
        mesh=mesh,
        in_specs=placed,
        out_specs=(P("dp", "tensor"), P("dp", None, "tensor")),
        check_vma=False,
    )
```

time: 635 us -> 97.6 us (0.15)
  waiting for transfers between devices: 538 us -> 0 us
  Pallas kernels: 0 us -> 89.5 us
  blocking collectives: 48.1 us -> 0 us
  matrix products: 17 us -> 0 us
  between operations: 13.9 us -> 0.67 us
  other arithmetic: 10.5 us -> 0 us
    all_gather x5 -> x0, waiting for transfers between devices: 536 us -> none  [the longest x1 155 us: on_device(): lax.all_gather(local_query, 'dp', axis=0, tiled=True)]
    pallas_call x0 -> x1, Pallas kernels: none -> 89.5 us  [on_device(): pl.pallas_call(kernel, out_shape=(jax.ShapeDtypeStruct((TOK, 4 * HD), BF1...]
    all_gather x2 -> x0, blocking collectives: 48.1 us -> none  [the longest x1 24.8 us: on_device(): lax.all_gather(value_weight, 'tensor', axis=0, tiled=True)]
    dot_general x5 -> x0, matrix products: 17 us -> none  [the longest x3 16.3 us: add_rows(): return jnp.dot(normed, shard_rows, preferred_element_type=jnp.float32)]
  transfers between devices with their start and end apart: 5 -> 0, of which waited for: 5 -> 0; matrix products, arithmetic and copies ran while one was open for 4% -> 0% of each run, Pallas kernels for 0% -> 0%
where the time goes in v1:
time: 97.6 us; the launch traced here: 97.2 us
  Pallas kernels  89.5 us (92%)
  local copies, waits for them, and re-layouts  6.95 us (7%)
    pallas_call x1, Pallas kernels, on_device(): pl.pallas_call(kernel, out_shape=(jax.ShapeDtypeStruct((TOK, 4 * HD), BF1...  89.5 us
    unnamed x22, local copies, waits for them, and re-layouts  6.94 us

profile of v1, /device:TPU:1, one launch (start us, length us, event | category | flops | bytes accessed | tf_op | source)
XLA Modules:
  0.0 97.2 jit_solution(1398927229620779928)
XLA Ops:
  0.6 0.0 copy-start.9
  0.6 0.7 copy-done.9
  1.3 0.0 copy-start.5
  1.3 0.0 copy-start.6
  1.3 0.0 copy-start.7
  1.3 0.0 copy-start.8
  1.3 0.6 copy-done.5
  2.0 0.0 copy-done.6
  2.0 0.0 copy-done.7
  2.0 0.0 copy-done.8
  2.0 0.0 copy-start
  2.0 1.0 %copy-done = bf16[256,1024]{1,0:T(8,128)(2,1)S(1)} copy-done((bf16[256,1024]{1,0:T(8,128)(2,1)S(1)}, bf16[256,1024]{1,0:T(8,128)(2,1)}, u32[]{:S(2)}) %copy-start) | copy-done | bytes 524312
  3.1 0.0 copy-start.1
  3.1 0.9 copy-done.1
  4.0 0.0 copy-start.2
  4.0 0.8 copy-done.2
  4.7 0.0 copy-start.3
  4.7 0.8 copy-done.3
  5.5 0.0 copy-start.4
  5.5 0.7 copy-done.4
  6.2 89.5 %handover.1 = (bf16[256,512]{1,0:T(8,128)(2,1)S(1)}, bf16[512,256]{1,0:T(8,128)(2,1)S(1)}) custom-call(bf16[256,1024]{1,0:T(8,128)(2,1)S(1)} %copy-done, bf16[64,128]{1,0:T(8,128)(2,1)S(1)} %bitcast.5, bf16[16,4096]{1,0:T(8,128)(2,1)S(1)} %copy-done.1, bf16[16,1024]{1,0:T(8,128)(2,1)S(1)} %copy-done.2, bf16[16,1024]{1,0:T(8,128)(2,1)S(1)} %copy-done.3, ...), custom_call_target="tpu_custom_call" | custom-call | tf_op jit(solution)/shard_map/handover/pallas_call | solution.py:325
  95.8 0.7 copy.14
  96.5 0.7 copy.15
  (1 shorter events, 0.0 us)
Async XLA Ops:
  0.6 0.7 copy-start.9
  1.3 0.7 copy-start.5
  1.3 0.7 copy-start.6
  1.3 0.7 copy-start.7
  1.3 0.7 copy-start.8
  2.0 1.0 %copy-start = (bf16[256,1024]{1,0:T(8,128)(2,1)S(1)}, bf16[256,1024]{1,0:T(8,128)(2,1)}, u32[]{:S(2)}) copy-start(bf16[256,1024]{1,0:T(8,128)(2,1)} %h_ref.1) | copy-start | bytes 1572868
  3.1 0.9 copy-start.1
  4.0 0.8 copy-start.2
  4.7 0.8 copy-start.3
  5.5 0.7 copy-start.4

commit v2 on v1

--- a/solution.py
+++ b/solution.py
@@ -21,6 +21,8 @@
 F32 = jnp.float32
 BF16 = jnp.bfloat16
 NEG = -1e30
+LATE = (0, 0, 3)
+SPLIT = (2, 2, 4)
 
 
 def rem(a, n):
@@ -28,8 +30,9 @@
 
 
 def kernel(
-    h_ref, gain_ref, wq_ref, wk_ref, wv_ref, bq_ref, bk_ref, bv_ref, len_ref, pt_ref,
+    h_in, gain_in, wq_in, wk_in, wv_in, bq_in, bk_in, bv_in, len_ref, pt_ref,
     att_ref, page_ref,
+    h_ref, gain_ref, wq_ref, wk_ref, wv_ref, bq_ref, bk_ref, bv_ref, in_sem,
     ws, wb, hs, a5, a2, ps, rs, ssb, cos_t, sin_t, mask_t, hot_t, kv_t,
     ws_send, ws_send_self, ws_recv, z_send, z_recv, c_send, c_recv, h_send, h_recv, p_send, p_recv, s_send, s_recv,
 ):
@@ -43,6 +46,14 @@
 
     def flip(bit, by):
         return rem(bit + by, 2)
+
+    def bring(i):
+        src = (gain_in, wq_in, wk_in, wv_in, h_in, bq_in, bk_in, bv_in)[i]
+        dst = (gain_ref, wq_ref, wk_ref, wv_ref, h_ref, bq_ref, bk_ref, bv_ref)[i]
+        return pltpu.make_async_copy(src, dst, in_sem.at[i])
+
+    for i in range(8):
+        bring(i).start()
 
     barrier = pltpu.get_barrier_semaphore()
     peers = []
@@ -54,6 +65,8 @@
     for d in peers:
         pl.semaphore_signal(barrier, inc=1, device_id=d, device_id_type=MESH)
 
+    for i in range(4):
+        bring(i).wait()
     g = gain_ref[...].astype(F32)
     g_row = jnp.sum(jnp.where(lax.broadcasted_iota(jnp.int32, g.shape, 0) == dp, g, 0.0), axis=0, keepdims=True)
     lane = lax.broadcasted_iota(jnp.int32, (16, 128), 1)
@@ -71,6 +84,8 @@
                         ws[(yh_d * 2 + yl_d) * 2 + k, j, :, 128 * e : 128 * e + 128] = (
                             parts[j].astype(F32) * g_col
                         ).astype(BF16)
+    for i in range(4, 8):
+        bring(i).wait()
     for b in range(2):
         for u in range(4):
             hs[b, u] = h_ref[:, 256 * u + 128 * b : 256 * u + 128 * b + 128]
@@ -131,9 +146,18 @@
         remote(wb.at[j, me, at, :], wb.at[j, me, at, :], c_send, c_recv.at[j], dev(x, y_lo, y_hi, z, other))
 
     wait(wb.at[:, me, rows(0, 0), :], ws_recv)
-    for j in range(2):
-        for way in range(2):
-            z_copy(way, j, rows(0, 0), rows(1, way), j, 1)
+    subs = []
+    for j in range(3):
+        n = 128 // SPLIT[j]
+        subs += [(j, n * q, n) for q in range(SPLIT[j])]
+
+    def own(cycle):
+        for si, (j, lo_row, n) in enumerate(subs):
+            if LATE[j] == cycle:
+                for way in range(2):
+                    z_copy(way, j, rows(0, 0, lo_row, n), rows(1, way, lo_row, n), si, 1)
+
+    own(0)
 
     h = h_ref[...].astype(F32)
     sq = h * h
@@ -219,46 +243,44 @@
         return run
 
     P_ = functools.partial
-    groups = (
-        ([(0, 0, 128), (1, 0, 128)], {1: first_tables, 3: page_tables}),
-        (
-            [(2, 0, 64), (2, 64, 64)],
-            {
-                1: both([wait_hidden, P_(relay, 0)]),
-                2: both([P_(relay, 1), P_(product, 0, 0)]),
-                3: both([P_(product, 0, 1), P_(send_parts, 0)]),
-                4: P_(product, 1, 0),
-                5: both([P_(product, 1, 1), P_(send_parts, 1)]),
-            },
-        ),
-    )
-    for gi, (subs, tasks) in enumerate(groups):
-        for step in range(1, 9):
-            for si, (j, lo_row, n) in enumerate(subs):
+    tasks = {1: [first_tables], 3: [page_tables], 6: [wait_hidden, P_(relay, 0)], 7: [P_(relay, 1)]}
+    last = max(LATE) + 8
+    queue = []
+    for cycle in range(1, last + 1):
+        for si, (j, lo_row, n) in enumerate(subs):
+            step = cycle - LATE[j]
+            if not 1 <= step <= 8:
+                continue
+            half = n // 2
+            for way in range(2):
+                sem = z_recv.at[way, si, step - 1]
+                lo2 = lo_row + way * half
+                if step < 8:
+                    at = rows(step, way, lo_row, n)
+                    wait(wb.at[j, me, at, :], sem)
+                    if step < 7:
+                        z_copy(way, j, at, rows(step + 1, way, lo_row, n), si, step + 1)
+                    else:
+                        z_copy(way, j, rows(7, way, lo2, half), rows(0, 1, lo2, half), si, 8)
+                else:
+                    wait(wb.at[j, me, rows(0, 1, lo2, half), :], sem)
+        own(cycle)
+        for j in range(3):
+            step = cycle - LATE[j]
+            if 1 <= step < 8:
                 for way in range(2):
-                    sem = z_recv.at[way, 2 * gi + si, step - 1]
-                    if step < 8:
-                        at = rows(step, way, lo_row, n)
-                        wait(wb.at[j, me, at, :], sem)
-                        if step < 7:
-                            z_copy(way, j, at, rows(step + 1, way, lo_row, n), 2 * gi + si, step + 1)
-                        elif gi == 0 or way == si:
-                            half = way * 64
-                            z_copy(way, j, rows(7, way, half, 64), rows(0, 1, half, 64), 2 * gi + si, 8)
-                        to_core(j, at)
-                    elif gi == 0 or way == si:
-                        at = rows(0, 1, way * 64, 64)
-                        wait(wb.at[j, me, at, :], sem)
-                        to_core(j, at)
-            if step == 7 and gi == 0:
-                for si, (j, lo_row, n) in enumerate(groups[1][0]):
-                    for way in range(2):
-                        z_copy(way, j, rows(0, 0, lo_row, n), rows(1, way, lo_row, n), 2 + si, 1)
-            if step in tasks:
-                tasks[step]()
-    product(2, 0)
-    product(2, 1)
-    send_parts(2)
+                    to_core(j, rows(step, way))
+            if step == 8:
+                to_core(j, rows(0, 1))
+                queue += [P_(product, j, 0), both([P_(product, j, 1), P_(send_parts, j)])]
+        if cycle in tasks:
+            for f in tasks[cycle]:
+                f()
+        elif cycle < last:
+            for _ in range(min(2, len(queue))):
+                queue.pop(0)()
+    for f in queue:
+        f()
 
     wait(ssb.at[pl.ds(1, 7)], s_recv)
     total = ssb[0, 0:1, :]
@@ -292,7 +314,7 @@
     page_ref[...] = jnp.dot(hot_t[...], kv_t[...], preferred_element_type=F32).astype(BF16)
 
     def attend(head, q):
-        q = rope(q + bq_ref[:, 128 * head : 128 * head + 128].astype(F32))
+        q = rope(q + bq_ref[head : head + 1].astype(F32))
         s = lax.dot_general(q, kv_t[:, 0:128], nt, preferred_element_type=F32) * HD ** (-0.5) + mask_t[...]
         w = jnp.exp(s - jnp.max(s, axis=-1, keepdims=True))
         w = (w / jnp.sum(w, axis=-1, keepdims=True)).astype(BF16)
@@ -319,6 +341,7 @@
 
 
 def on_device(hidden, gain, wq, wk, wv, bq, bk, bv, lengths, table):
+    hbm = pl.BlockSpec(memory_space=pltpu.MemorySpace.HBM)
     vmem = pl.BlockSpec(memory_space=pltpu.VMEM)
     smem = pl.BlockSpec(memory_space=pltpu.SMEM)
     dma = pltpu.SemaphoreType.DMA
@@ -328,9 +351,14 @@
             jax.ShapeDtypeStruct((TOK, 4 * HD), BF16),
             jax.ShapeDtypeStruct((PAGES_REP * PAGE, 2 * HD), BF16),
         ),
-        in_specs=[vmem] * 8 + [smem] * 2,
+        in_specs=[hbm] * 8 + [smem] * 2,
         out_specs=(vmem, vmem),
         scratch_shapes=[
+            *[
+                pltpu.VMEM(s, BF16)
+                for s in ((TOK, 1024), (64, 128), (16, 4096), (16, 1024), (16, 1024), (4, 128), (1, 128), (1, 128))
+            ],
+            dma((8,)),
             pltpu.VMEM((8, 3, 16, 256), BF16),
             pltpu.VMEM((3, 2, 2048, 256), BF16),
             pltpu.VMEM((2, 4, TOK, 128), BF16),
@@ -344,14 +372,14 @@
             pltpu.VMEM((TOK, TOK), F32),
             pltpu.VMEM((PAGES_REP * PAGE, TOK), BF16),
             pltpu.VMEM((TOK, 256), BF16),
-            dma, dma, dma, dma, dma((2, 4, 8)), dma, dma((3,)), dma, dma, dma, dma((3,)), dma, dma,
+            dma, dma, dma, dma, dma((2, 8, 8)), dma, dma((3,)), dma, dma, dma, dma((3,)), dma, dma,
         ],
         compiler_params=pltpu.CompilerParams(
-            collective_id=0, has_side_effects=True, vmem_limit_bytes=40 * 2**20
+            collective_id=0, has_side_effects=True, vmem_limit_bytes=60 * 2**20
         ),
         name="handover",
     )(
-        hidden, gain.reshape(64, 128), wq, wk, wv, bq.reshape(1, -1), bk.reshape(1, -1), bv.reshape(1, -1),
+        hidden, gain.reshape(64, 128), wq, wk, wv, bq.reshape(4, -1), bk.reshape(1, -1), bv.reshape(1, -1),
         lengths, table,
     )
     return att, pages.reshape(PAGES_REP, PAGE, 2 * HD)

time: 97.6 us -> 83.6 us (0.86)
  Pallas kernels: 89.5 us -> 80.4 us
  local copies, waits for them, and re-layouts: 6.95 us -> 2.42 us
    pallas_call x1, Pallas kernels: 89.5 us -> 80.4 us  [on_device(): pl.pallas_call(kernel, out_shape=(jax.ShapeDtypeStruct((TOK, 4 * HD), BF1...]
    unnamed x22 -> x4, local copies, waits for them, and re-layouts: 6.94 us -> 2.42 us
where the time goes in v2:
time: 83.6 us; the launch traced here: 83.4 us
  Pallas kernels  80.4 us (96%)
  local copies, waits for them, and re-layouts  2.42 us (3%)
    pallas_call x1, Pallas kernels, on_device(): pl.pallas_call(kernel, out_shape=(jax.ShapeDtypeStruct((TOK, 4 * HD), BF1...  80.4 us
    unnamed x4, local copies, waits for them, and re-layouts  2.42 us

profile of v2, /device:TPU:1, one launch (start us, length us, event | category | flops | bytes accessed | tf_op | source)
XLA Modules:
  0.0 83.4 jit_solution(18372206575073990968)
XLA Ops:
  0.6 80.4 %handover.1 = (bf16[256,512]{1,0:T(8,128)(2,1)}, bf16[512,256]{1,0:T(8,128)(2,1)}) custom-call(bf16[256,1024]{1,0:T(8,128)(2,1)} %h_in.1, bf16[64,128]{1,0:T(8,128)(2,1)} %bitcast.6, bf16[16,4096]{1,0:T(8,128)(2,1)} %wq_in.1, bf16[16,1024]{1,0:T(8,128)(2,1)} %wk_in.1, bf16[16,1024]{1,0:T(8,128)(2,1)} %wv_in.1, bf16[4,128]{1,0:T(4,128)(2,1)} %bitcast.7, ...), custom_call_target="tpu_custom_call" | custom-call | tf_op jit(solution)/shard_map/handover/pallas_call | solution.py:348
  81.0 0.0 copy-start
  81.0 1.7 %copy.14 = bf16[256,512]{1,0:T(8,128)(2,1)} copy(bf16[256,512]{1,0:T(8,128)(2,1)} %get-tuple-element.8) | data formatting | bytes 524288
  82.7 0.0 copy-done
  82.7 0.7 copy.15
Async XLA Ops:
  81.0 1.7 %copy-start = (bf16[512,256]{1,0:T(8,128)(2,1)S(1)}, bf16[512,256]{1,0:T(8,128)(2,1)}, u32[]{:S(2)}) copy-start(bf16[512,256]{1,0:T(8,128)(2,1)} %get-tuple-element.5) | copy-start | bytes 786436

commit v3 on v2

--- a/solution.py
+++ b/solution.py
@@ -23,6 +23,7 @@
 NEG = -1e30
 LATE = (0, 0, 3)
 SPLIT = (2, 2, 4)
+U = 3
 
 
 def rem(a, n):
@@ -33,7 +34,7 @@
     h_in, gain_in, wq_in, wk_in, wv_in, bq_in, bk_in, bv_in, len_ref, pt_ref,
     att_ref, page_ref,
     h_ref, gain_ref, wq_ref, wk_ref, wv_ref, bq_ref, bk_ref, bv_ref, in_sem,
-    ws, wb, hs, a5, a2, ps, rs, ssb, cos_t, sin_t, mask_t, hot_t, kv_t,
+    ws, wb, a5, a2, ps, rs, ssb, cos_t, sin_t, mask_t, hot_t, kv_t,
     ws_send, ws_send_self, ws_recv, z_send, z_recv, c_send, c_recv, h_send, h_recv, p_send, p_recv, s_send, s_recv,
 ):
     dp = lax.axis_index("dp")
@@ -76,7 +77,7 @@
         for yl_d in range(2):
             for k in range(2):
                 for e in range(2):
-                    td = 4 * k + 2 * e + yl_d
+                    td = 4 * e + 2 * k + yl_d
                     first = (wk_ref if yh_d == 0 else wv_ref)[:, 128 * td : 128 * td + 128]
                     q0 = 512 * td + 256 * yh_d
                     parts = (first, wq_ref[:, q0 : q0 + 128], wq_ref[:, q0 + 128 : q0 + 256])
@@ -86,9 +87,10 @@
                         ).astype(BF16)
     for i in range(4, 8):
         bring(i).wait()
-    for b in range(2):
-        for u in range(4):
-            hs[b, u] = h_ref[:, 256 * u + 128 * b : 256 * u + 128 * b + 128]
+    x0, x1 = rem(x, 2), x // 2
+    piece = (y_hi * 4 + rem(t, 4)) * 8
+    for u in range(8):
+        a5[piece + u] = h_ref[:, 128 * u : 128 * u + 128]
 
     pl.semaphore_wait(barrier, len(peers))
 
@@ -100,35 +102,82 @@
     def wait(ref, sem):
         pltpu.make_async_copy(ref, ref, sem).wait()
 
-    x_dst = 2 * y_hi + core
     slot_w = pl.ds(pl.multiple_of(16 * t, 16), 16)
     for r in range(8):
-        yl_d, yh_d, k = flip(y_lo, r % 2), flip(y_hi, r // 2 % 2), flip(core, r // 4)
+        yl_d, yh_d, k = flip(y_lo, r % 2), flip(y_hi, r // 2 % 2), flip(x0, r // 4)
         src = ws.at[(yh_d * 2 + yl_d) * 2 + k]
-        dst = wb.at[:, k, slot_w, :]
-        to = dev(x_dst, yl_d, yh_d, z, k)
+        dst = wb.at[:, core, slot_w, :]
+        to = dev(2 * y_hi + k, yl_d, yh_d, z, core)
         if r > 0:
             remote(src, dst, ws_send, ws_recv, to)
         else:
 
-            @pl.when(x == x_dst)
+            @pl.when(x1 == y_hi)
             def _():
                 pltpu.make_async_copy(src, dst, ws_recv).start()
 
-            @pl.when(x != x_dst)
+            @pl.when(x1 != y_hi)
             def _():
                 remote(src, dst, ws_send_self, ws_recv, to)
 
-    xb = rem(x, 2)
-    x_pair = x + 1 - 2 * xb
-    piece = 4 * (y_hi * 4 + rem(t, 4))
-    for r in (1, 2, 3, 4, 5, 6, 7):
-        xd = x if r < 4 else x_pair
-        src = hs.at[xb if r < 4 else 1 - xb]
-        to = dev(xd, flip(y_lo, r % 2), flip(y_hi, r // 2 % 2), z, core)
-        remote(src, a5.at[pl.ds(piece, 4)], h_send, h_recv, to)
-    for u in range(4):
-        a5[piece + u] = hs[xb, u]
+    pair = dev(2 * x1 + 1 - x0, y_lo, y_hi, z, core)
+    pair_piece = (y_hi * 4 + 2 * (1 - x0) + y_lo) * 8
+
+    def row(r):
+        return flip(y_lo, r % 2), flip(y_hi, r // 2)
+
+    def move(base, lo, n, sem, to):
+        at = a5.at[pl.ds(base + lo, n)]
+        remote(at, at, h_send, h_recv.at[sem], to)
+
+    def own_x(lo, n, sem):
+        move(piece, lo, n, sem, pair)
+
+    def own_y(r, lo, n, sem):
+        yl, yh = row(r)
+        move(piece, lo, n, sem, dev(x, yl, yh, z, core))
+
+    def pair_y(r):
+        yl, yh = row(r)
+        move(pair_piece, 0, U, 5, dev(x, yl, yh, z, core))
+
+    def got(n, sem):
+        wait(a5.at[pl.ds(0, n)], h_recv.at[sem])
+
+    def pass_x(r):
+        got(8 - U, 1 + r)
+        yl, yh = row(r)
+        move((yh * 4 + 2 * x0 + yl) * 8, U, 8 - U, 7, pair)
+
+    own_x(0, U, 0)
+    for r in (1, 3):
+        own_y(r, U, 8 - U, 1 + r)
+
+    def hidden_0():
+        own_x(U, 8 - U, 1)
+        got(U, 0)
+        pair_y(1)
+        pair_y(3)
+
+    def hidden_1():
+        own_y(2, U, 8 - U, 3)
+        pass_x(1)
+        pass_x(3)
+
+    def hidden_2():
+        own_y(1, 0, U, 6)
+        own_y(3, 0, U, 6)
+
+    def hidden_4():
+        own_y(2, 0, U, 6)
+        pair_y(2)
+        pass_x(2)
+
+    def wait_hidden():
+        got(8 - U, 1)
+        got(3 * U, 5)
+        got(3 * U, 6)
+        got(3 * (8 - U), 7)
 
     me = core
     other = 1 - core
@@ -158,6 +207,7 @@
                     z_copy(way, j, rows(0, 0, lo_row, n), rows(1, way, lo_row, n), si, 1)
 
     own(0)
+    hidden_0()
 
     h = h_ref[...].astype(F32)
     sq = h * h
@@ -210,40 +260,34 @@
         for q in range(2):
             hot_t[:, 128 * q : 128 * q + 128] = jnp.where(src == col + 128 * q, 1.0, 0.0).astype(BF16)
 
-    def wait_hidden():
-        wait(a5.at[pl.ds(0, 28)], h_recv)
-
-    def relay(tk):
+    def relay(tk, k):
         for p in range(8):
             m1 = rem(z + NZ - p, NZ)
             m2 = rem(z + p, NZ) if p else rem(z + 8, NZ)
-            a2[tk, :, 256 * p : 256 * p + 128] = a5[tk * NZ + m1]
-            a2[tk, :, 256 * p + 128 : 256 * p + 256] = a5[tk * NZ + m2]
-
-    def product(j, k):
-        if k == 0:
+            a2[tk, k, :, 256 * p : 256 * p + 128] = a5[tk * 32 + 2 * m1 + k]
+            a2[tk, k, :, 256 * p + 128 : 256 * p + 256] = a5[tk * 32 + 2 * m2 + k]
+
+    def product(j, far):
+        tk = 1 - y_hi if far else y_hi
+        if far:
             wait(wb.at[j, other], c_recv.at[j])
-
-        @pl.loop(0, 2)
-        def _(tk):
-            part = jnp.dot(a2[tk], wb[j, k], preferred_element_type=F32).astype(BF16)
-            for e in range(2):
-                ps[j, tk * 4 + 2 * k + e] = part[:, 128 * e : 128 * e + 128]
-
-    def send_parts(j):
-        for r in range(7, 0, -1):
-            xd, yh_d = rem(x + r % 4, 4), flip(y_hi, r // 4)
-            remote(ps.at[j, yh_d * 4 + xd], rs.at[j, r], p_send, p_recv.at[j], dev(xd, y_lo, yh_d, z, core))
-
-    def both(tasks):
-        def run():
-            for f in tasks:
-                f()
-
-        return run
+        part = jnp.dot(a2[tk, 0], wb[j, 0], preferred_element_type=F32) + jnp.dot(
+            a2[tk, 1], wb[j, 1], preferred_element_type=F32
+        )
+        part = part.astype(BF16)
+        for e in range(2):
+            ps[j, tk * 2 + e] = part[:, 128 * e : 128 * e + 128]
+        for r in (3, 2) if far else (1,):
+            e = flip(x1, r % 2)
+            remote(
+                ps.at[j, tk * 2 + e], rs.at[j, r], p_send, p_recv.at[j], dev(2 * e + x0, y_lo, tk, z, core)
+            )
 
     P_ = functools.partial
-    tasks = {1: [first_tables], 3: [page_tables], 6: [wait_hidden, P_(relay, 0)], 7: [P_(relay, 1)]}
+    tasks = {
+        1: [hidden_1], 2: [hidden_2, first_tables], 3: [page_tables], 4: [hidden_4],
+        7: [wait_hidden, P_(relay, 0, 0), P_(relay, 0, 1)], 8: [P_(relay, 1, 0), P_(relay, 1, 1)],
+    }
     last = max(LATE) + 8
     queue = []
     for cycle in range(1, last + 1):
@@ -272,7 +316,7 @@
                     to_core(j, rows(step, way))
             if step == 8:
                 to_core(j, rows(0, 1))
-                queue += [P_(product, j, 0), both([P_(product, j, 1), P_(send_parts, j)])]
+                queue += [P_(product, j, True), P_(product, j, False)]
         if cycle in tasks:
             for f in tasks[cycle]:
                 f()
@@ -291,13 +335,9 @@
     scale = jnp.sum(jnp.where(eye, scale_row, 0.0), axis=1, keepdims=True)
 
     def gathered(j):
-        wait(rs.at[j, pl.ds(1, 7)], p_recv.at[j])
-        own = ps[j, y_hi * 4 + x].astype(F32)
-        for r in range(1, 4):
-            own = own + rs[j, r].astype(F32)
-        far = rs[j, 4].astype(F32)
-        for r in range(5, 8):
-            far = far + rs[j, r].astype(F32)
+        wait(rs.at[j, pl.ds(1, 3)], p_recv.at[j])
+        own = ps[j, y_hi * 2 + x1].astype(F32) + rs[j, 1].astype(F32)
+        far = rs[j, 2].astype(F32) + rs[j, 3].astype(F32)
         return (
             jnp.where(y_hi == 0, own, far) * scale,
             jnp.where(y_hi == 0, far, own) * scale,
@@ -329,15 +369,15 @@
 
     wait(ws.at[pl.ds(0, 7)], ws_send)
 
-    @pl.when(x != x_dst)
+    @pl.when(x1 != y_hi)
     def _():
         wait(ws.at[0], ws_send_self)
 
-    wait(a5.at[pl.ds(0, 28)], h_send)
+    wait(a5.at[pl.ds(0, 56)], h_send)
     wait(ssb.at[pl.ds(1, 7)], s_send)
     wait(wb.at[:, 0, pl.ds(0, 1920), :], z_send)
     wait(wb.at[:, 0], c_send)
-    wait(rs.at[:, pl.ds(1, 7)], p_send)
+    wait(rs.at[:, pl.ds(1, 3)], p_send)
 
 
 def on_device(hidden, gain, wq, wk, wv, bq, bk, bv, lengths, table):
@@ -361,18 +401,17 @@
             dma((8,)),
             pltpu.VMEM((8, 3, 16, 256), BF16),
             pltpu.VMEM((3, 2, 2048, 256), BF16),
-            pltpu.VMEM((2, 4, TOK, 128), BF16),
-            pltpu.VMEM((32, TOK, 128), BF16),
-            pltpu.VMEM((2, TOK, 2048), BF16),
-            pltpu.VMEM((3, 8, TOK, 128), BF16),
-            pltpu.VMEM((3, 8, TOK, 128), BF16),
+            pltpu.VMEM((64, TOK, 128), BF16),
+            pltpu.VMEM((2, 2, TOK, 2048), BF16),
+            pltpu.VMEM((3, 4, TOK, 128), BF16),
+            pltpu.VMEM((3, 4, TOK, 128), BF16),
             pltpu.VMEM((8, 8, TOK), F32),
             pltpu.VMEM((TOK, 128), F32),
             pltpu.VMEM((TOK, 128), F32),
             pltpu.VMEM((TOK, TOK), F32),
             pltpu.VMEM((PAGES_REP * PAGE, TOK), BF16),
             pltpu.VMEM((TOK, 256), BF16),
-            dma, dma, dma, dma, dma((2, 8, 8)), dma, dma((3,)), dma, dma, dma, dma((3,)), dma, dma,
+            dma, dma, dma, dma, dma((2, 8, 8)), dma, dma((3,)), dma, dma((8,)), dma, dma((3,)), dma, dma,
         ],
         compiler_params=pltpu.CompilerParams(
             collective_id=0, has_side_effects=True, vmem_limit_bytes=60 * 2**20

time: 83.6 us -> 79.9 us (0.956)
  Pallas kernels: 80.4 us -> 76.6 us
    pallas_call x1, Pallas kernels: 80.4 us -> 76.6 us  [on_device(): pl.pallas_call(kernel, out_shape=(jax.ShapeDtypeStruct((TOK, 4 * HD), BF1...]
where the time goes in v3:
time: 79.9 us; the launch traced here: 79.7 us
  Pallas kernels  76.6 us (96%)
  local copies, waits for them, and re-layouts  2.42 us (3%)
    pallas_call x1, Pallas kernels, on_device(): pl.pallas_call(kernel, out_shape=(jax.ShapeDtypeStruct((TOK, 4 * HD), BF1...  76.6 us
    unnamed x4, local copies, waits for them, and re-layouts  2.42 us

profile of v3, /device:TPU:1, one launch (start us, length us, event | category | flops | bytes accessed | tf_op | source)
XLA Modules:
  0.0 79.7 jit_solution(15623293113981496875)
XLA Ops:
  0.6 76.6 %handover.1 = (bf16[256,512]{1,0:T(8,128)(2,1)}, bf16[512,256]{1,0:T(8,128)(2,1)}) custom-call(bf16[256,1024]{1,0:T(8,128)(2,1)} %h_in.1, bf16[64,128]{1,0:T(8,128)(2,1)} %bitcast.6, bf16[16,4096]{1,0:T(8,128)(2,1)} %wq_in.1, bf16[16,1024]{1,0:T(8,128)(2,1)} %wk_in.1, bf16[16,1024]{1,0:T(8,128)(2,1)} %wv_in.1, bf16[4,128]{1,0:T(4,128)(2,1)} %bitcast.7, ...), custom_call_target="tpu_custom_call" | custom-call | tf_op jit(solution)/shard_map/handover/pallas_call | solution.py:388
  77.3 0.0 copy-start
  77.3 1.7 %copy.14 = bf16[256,512]{1,0:T(8,128)(2,1)} copy(bf16[256,512]{1,0:T(8,128)(2,1)} %get-tuple-element.8) | data formatting | bytes 524288
  79.0 0.0 copy-done
  79.0 0.7 copy.15
Async XLA Ops:
  77.3 1.7 %copy-start = (bf16[512,256]{1,0:T(8,128)(2,1)S(1)}, bf16[512,256]{1,0:T(8,128)(2,1)}, u32[]{:S(2)}) copy-start(bf16[512,256]{1,0:T(8,128)(2,1)} %get-tuple-element.5) | copy-start | bytes 786436

commit v4 on v3

--- a/solution.py
+++ b/solution.py
@@ -21,8 +21,9 @@
 F32 = jnp.float32
 BF16 = jnp.bfloat16
 NEG = -1e30
-LATE = (0, 0, 3)
-SPLIT = (2, 2, 4)
+LATE = (0, 1, 1)
+SPLIT = (2, 2, 2)
+WH = 7
 U = 3
 
 
@@ -82,15 +83,10 @@
                     q0 = 512 * td + 256 * yh_d
                     parts = (first, wq_ref[:, q0 : q0 + 128], wq_ref[:, q0 + 128 : q0 + 256])
                     for j in range(3):
-                        ws[(yh_d * 2 + yl_d) * 2 + k, j, :, 128 * e : 128 * e + 128] = (
+                        ws[j, (yh_d * 2 + yl_d) * 2 + k, :, 128 * e : 128 * e + 128] = (
                             parts[j].astype(F32) * g_col
                         ).astype(BF16)
-    for i in range(4, 8):
-        bring(i).wait()
     x0, x1 = rem(x, 2), x // 2
-    piece = (y_hi * 4 + rem(t, 4)) * 8
-    for u in range(8):
-        a5[piece + u] = h_ref[:, 128 * u : 128 * u + 128]
 
     pl.semaphore_wait(barrier, len(peers))
 
@@ -103,22 +99,33 @@
         pltpu.make_async_copy(ref, ref, sem).wait()
 
     slot_w = pl.ds(pl.multiple_of(16 * t, 16), 16)
-    for r in range(8):
-        yl_d, yh_d, k = flip(y_lo, r % 2), flip(y_hi, r // 2 % 2), flip(x0, r // 4)
-        src = ws.at[(yh_d * 2 + yl_d) * 2 + k]
-        dst = wb.at[:, core, slot_w, :]
-        to = dev(2 * y_hi + k, yl_d, yh_d, z, core)
-        if r > 0:
-            remote(src, dst, ws_send, ws_recv, to)
-        else:
-
-            @pl.when(x1 == y_hi)
-            def _():
-                pltpu.make_async_copy(src, dst, ws_recv).start()
-
-            @pl.when(x1 != y_hi)
-            def _():
-                remote(src, dst, ws_send_self, ws_recv, to)
+
+    def shuffle(j):
+        for r in range(8):
+            yl_d, yh_d, k = flip(y_lo, r % 2), flip(y_hi, r // 2 % 2), flip(x0, r // 4)
+            src = ws.at[j, (yh_d * 2 + yl_d) * 2 + k]
+            dst = wb.at[j, core, slot_w, :]
+            to = dev(2 * y_hi + k, yl_d, yh_d, z, core)
+            if r > 0:
+                remote(src, dst, ws_send, ws_recv.at[j], to)
+            else:
+
+                @pl.when(x1 == y_hi)
+                def _():
+                    pltpu.make_async_copy(src, dst, ws_recv.at[j]).start()
+
+                @pl.when(x1 != y_hi)
+                def _():
+                    remote(src, dst, ws_send_self, ws_recv.at[j], to)
+
+    for j in range(3):
+        shuffle(j)
+
+    for i in range(4, 8):
+        bring(i).wait()
+    piece = (y_hi * 4 + rem(t, 4)) * 8
+    for u in range(8):
+        a5[piece + u] = h_ref[:, 128 * u : 128 * u + 128]
 
     pair = dev(2 * x1 + 1 - x0, y_lo, y_hi, z, core)
     pair_piece = (y_hi * 4 + 2 * (1 - x0) + y_lo) * 8
@@ -194,7 +201,6 @@
     def to_core(j, at):
         remote(wb.at[j, me, at, :], wb.at[j, me, at, :], c_send, c_recv.at[j], dev(x, y_lo, y_hi, z, other))
 
-    wait(wb.at[:, me, rows(0, 0), :], ws_recv)
     subs = []
     for j in range(3):
         n = 128 // SPLIT[j]
@@ -203,6 +209,8 @@
     def own(cycle):
         for si, (j, lo_row, n) in enumerate(subs):
             if LATE[j] == cycle:
+                if lo_row == 0:
+                    wait(wb.at[j, me, rows(0, 0), :], ws_recv.at[j])
                 for way in range(2):
                     z_copy(way, j, rows(0, 0, lo_row, n), rows(1, way, lo_row, n), si, 1)
 
@@ -220,8 +228,6 @@
     )
     for r in range(1, 8):
         remote(ssb.at[0], ssb.at[r], s_send, s_recv, dev(rem(x + r % 4, 4), flip(y_lo, r // 4), y_hi, z, core))
-    for j in range(3):
-        to_core(j, rows(0, 0))
 
     def first_tables():
         ends, starts, total = [], [], 0
@@ -286,7 +292,7 @@
     P_ = functools.partial
     tasks = {
         1: [hidden_1], 2: [hidden_2, first_tables], 3: [page_tables], 4: [hidden_4],
-        7: [wait_hidden, P_(relay, 0, 0), P_(relay, 0, 1)], 8: [P_(relay, 1, 0), P_(relay, 1, 1)],
+        WH: [wait_hidden, P_(relay, 0, 0), P_(relay, 0, 1)], WH + 1: [P_(relay, 1, 0), P_(relay, 1, 1)],
     }
     last = max(LATE) + 8
     queue = []
@@ -311,6 +317,8 @@
         own(cycle)
         for j in range(3):
             step = cycle - LATE[j]
+            if step == 1:
+                to_core(j, rows(0, 0))
             if 1 <= step < 8:
                 for way in range(2):
                     to_core(j, rows(step, way))
@@ -367,11 +375,11 @@
         attend(j - 1, low)
         attend(j + 1, high)
 
-    wait(ws.at[pl.ds(0, 7)], ws_send)
+    wait(ws.at[:, pl.ds(0, 7)], ws_send)
 
     @pl.when(x1 != y_hi)
     def _():
-        wait(ws.at[0], ws_send_self)
+        wait(ws.at[:, 0], ws_send_self)
 
     wait(a5.at[pl.ds(0, 56)], h_send)
     wait(ssb.at[pl.ds(1, 7)], s_send)
@@ -399,7 +407,7 @@
                 for s in ((TOK, 1024), (64, 128), (16, 4096), (16, 1024), (16, 1024), (4, 128), (1, 128), (1, 128))
             ],
             dma((8,)),
-            pltpu.VMEM((8, 3, 16, 256), BF16),
+            pltpu.VMEM((3, 8, 16, 256), BF16),
             pltpu.VMEM((3, 2, 2048, 256), BF16),
             pltpu.VMEM((64, TOK, 128), BF16),
             pltpu.VMEM((2, 2, TOK, 2048), BF16),
@@ -411,7 +419,7 @@
             pltpu.VMEM((TOK, TOK), F32),
             pltpu.VMEM((PAGES_REP * PAGE, TOK), BF16),
             pltpu.VMEM((TOK, 256), BF16),
-            dma, dma, dma, dma, dma((2, 8, 8)), dma, dma((3,)), dma, dma((8,)), dma, dma((3,)), dma, dma,
+            dma, dma, dma((3,)), dma, dma((2, 6, 8)), dma, dma((3,)), dma, dma((8,)), dma, dma((3,)), dma, dma,
         ],
         compiler_params=pltpu.CompilerParams(
             collective_id=0, has_side_effects=True, vmem_limit_bytes=60 * 2**20

time: 79.9 us -> 76.7 us (0.960)
  Pallas kernels: 76.6 us -> 73.4 us
    pallas_call x1, Pallas kernels: 76.6 us -> 73.4 us  [on_device(): pl.pallas_call(kernel, out_shape=(jax.ShapeDtypeStruct((TOK, 4 * HD), BF1...]
where the time goes in v4:
time: 76.7 us; the launch traced here: 76.5 us
  Pallas kernels  73.4 us (96%)
  local copies, waits for them, and re-layouts  2.42 us (3%)
    pallas_call x1, Pallas kernels, on_device(): pl.pallas_call(kernel, out_shape=(jax.ShapeDtypeStruct((TOK, 4 * HD), BF1...  73.4 us
    unnamed x4, local copies, waits for them, and re-layouts  2.42 us

profile of v4, /device:TPU:1, one launch (start us, length us, event | category | flops | bytes accessed | tf_op | source)
XLA Modules:
  0.0 76.5 jit_solution(5980198683669078204)
XLA Ops:
  0.6 73.4 %handover.1 = (bf16[256,512]{1,0:T(8,128)(2,1)}, bf16[512,256]{1,0:T(8,128)(2,1)}) custom-call(bf16[256,1024]{1,0:T(8,128)(2,1)} %h_in.1, bf16[64,128]{1,0:T(8,128)(2,1)} %bitcast.6, bf16[16,4096]{1,0:T(8,128)(2,1)} %wq_in.1, bf16[16,1024]{1,0:T(8,128)(2,1)} %wk_in.1, bf16[16,1024]{1,0:T(8,128)(2,1)} %wv_in.1, bf16[4,128]{1,0:T(4,128)(2,1)} %bitcast.7, ...), custom_call_target="tpu_custom_call" | custom-call | tf_op jit(solution)/shard_map/handover/pallas_call | solution.py:396
  74.0 0.0 copy-start
  74.0 1.7 %copy.14 = bf16[256,512]{1,0:T(8,128)(2,1)} copy(bf16[256,512]{1,0:T(8,128)(2,1)} %get-tuple-element.8) | data formatting | bytes 524288
  75.8 0.0 copy-done
  75.8 0.7 copy.15
Async XLA Ops:
  74.0 1.7 %copy-start = (bf16[512,256]{1,0:T(8,128)(2,1)S(1)}, bf16[512,256]{1,0:T(8,128)(2,1)}, u32[]{:S(2)}) copy-start(bf16[512,256]{1,0:T(8,128)(2,1)} %get-tuple-element.5) | copy-start | bytes 786436

commit v5 on v4

--- a/solution.py
+++ b/solution.py
@@ -21,7 +21,7 @@
 F32 = jnp.float32
 BF16 = jnp.bfloat16
 NEG = -1e30
-LATE = (0, 1, 1)
+LATE = (0, 0, 1)
 SPLIT = (2, 2, 2)
 WH = 7
 U = 3
@@ -324,15 +324,15 @@
                     to_core(j, rows(step, way))
             if step == 8:
                 to_core(j, rows(0, 1))
-                queue += [P_(product, j, True), P_(product, j, False)]
-        if cycle in tasks:
-            for f in tasks[cycle]:
-                f()
-        elif cycle < last:
-            for _ in range(min(2, len(queue))):
-                queue.pop(0)()
-    for f in queue:
-        f()
+                queue += [(j, True), (j, False)]
+        for f in tasks.get(cycle, ()):
+            f()
+        if cycle == last - 1:
+            for j, far in queue:
+                product(j, far)
+            queue = []
+    for j, far in sorted(queue, key=lambda q: not q[1]):
+        product(j, far)
 
     wait(ssb.at[pl.ds(1, 7)], s_recv)
     total = ssb[0, 0:1, :]

time: 76.7 us -> 75.2 us (0.980)
  Pallas kernels: 73.4 us -> 72 us
    pallas_call x1, Pallas kernels: 73.4 us -> 72 us  [on_device(): pl.pallas_call(kernel, out_shape=(jax.ShapeDtypeStruct((TOK, 4 * HD), BF1...]
where the time goes in v5:
time: 75.2 us; the launch traced here: 75 us
  Pallas kernels  72 us (96%)
  local copies, waits for them, and re-layouts  2.42 us (3%)
    pallas_call x1, Pallas kernels, on_device(): pl.pallas_call(kernel, out_shape=(jax.ShapeDtypeStruct((TOK, 4 * HD), BF1...  72 us
    unnamed x4, local copies, waits for them, and re-layouts  2.42 us

profile of v5, /device:TPU:1, one launch (start us, length us, event | category | flops | bytes accessed | tf_op | source)
XLA Modules:
  0.0 75.0 jit_solution(17835011967306771215)
XLA Ops:
  0.6 72.0 %handover.1 = (bf16[256,512]{1,0:T(8,128)(2,1)}, bf16[512,256]{1,0:T(8,128)(2,1)}) custom-call(bf16[256,1024]{1,0:T(8,128)(2,1)} %h_in.1, bf16[64,128]{1,0:T(8,128)(2,1)} %bitcast.6, bf16[16,4096]{1,0:T(8,128)(2,1)} %wq_in.1, bf16[16,1024]{1,0:T(8,128)(2,1)} %wk_in.1, bf16[16,1024]{1,0:T(8,128)(2,1)} %wv_in.1, bf16[4,128]{1,0:T(4,128)(2,1)} %bitcast.7, ...), custom_call_target="tpu_custom_call" | custom-call | tf_op jit(solution)/shard_map/handover/pallas_call | solution.py:396
  72.6 0.0 copy-start
  72.6 1.7 %copy.14 = bf16[256,512]{1,0:T(8,128)(2,1)} copy(bf16[256,512]{1,0:T(8,128)(2,1)} %get-tuple-element.8) | data formatting | bytes 524288
  74.3 0.0 copy-done
  74.3 0.7 copy.15
Async XLA Ops:
  72.6 1.7 %copy-start = (bf16[512,256]{1,0:T(8,128)(2,1)S(1)}, bf16[512,256]{1,0:T(8,128)(2,1)}, u32[]{:S(2)}) copy-start(bf16[512,256]{1,0:T(8,128)(2,1)} %get-tuple-element.5) | copy-start | bytes 786436
